TPU v7x, 32 devices: a whole 2x2x4 slice. The times are simulated.
32 devices in a mesh: wave: 8 (over z, x), dof: 4 (over y, core).
Axes of the slice: x: 2, y: 2, z: 4, core: 2. Of those that a mesh axis runs over, the one named last changes fastest.
Arguments:
- green: bfloat16 [2, 2048, 512, 512], P(None, 'wave', None, 'dof'), may hold values from -0.25 to 0.25
- rough: float32 [2, 2048, 512], P(None, 'wave'), may hold values from -6 to 6
- axle_pos: int32 [128, 32], replicated, may hold values from 0 to 2047
- axle_load: float32 [128, 32], replicated, may hold values from 0.5 to 1.5
- rows: int32 [1024, 16], replicated, may hold values from 0 to 2047
- counts: int32 [1024], replicated, may hold values from 1 to 16, as said below
- coupling: bfloat16 [1024, 512], P(None, 'dof'), may hold values from -0.25 to 0.25
Outputs:
- response: float32 [1024, 128], P('dof', 'wave')
Inputs may be any that keep to these rules, and one draw needn't show every extreme that they name: Building b uses its first counts[b] stations; some building uses all 16.
All inputs are finite; a program needn't handle non-finite values.
Results may differ from a plain program's by a relative error of at most 0.005.
Values may be sent and summed in bfloat16 or wider, within the bound.
No kernel may reach another device: no remote copies, remote signals or barrier semaphores. Data moves between devices by JAX's collectives and lax.ppermute only.
A program may use at most 320 MiB of HBM per device.

v0:
```python
import math

import jax
import jax.numpy as jnp
from jax import lax
from jax.sharding import PartitionSpec as P

K = 2048


def make_table():
    stations = jnp.arange(K, dtype=jnp.int32)
    product = stations[:, None] * stations[None, :] % K
    angle = product.astype(jnp.float32) * (2.0 * math.pi / K)
    scale = 1.0 / math.sqrt(K)
    table = jnp.stack([jnp.cos(angle) * scale, -jnp.sin(angle) * scale], axis=2)
    return table.reshape(K, 2 * K).astype(jnp.bfloat16)


def building_terms(field, coupling_part, occupancy, counts):
    flat = field.reshape(field.shape[0], field.shape[1] * field.shape[2])
    gathered = jnp.dot(
        occupancy.astype(jnp.float32),
        flat,
        precision=lax.Precision.HIGHEST,
        preferred_element_type=jnp.float32,
    )
    gathered = gathered.reshape(occupancy.shape[0], field.shape[1], field.shape[2])
    summed = jnp.einsum(
        "bi,bic->bc", coupling_part.astype(jnp.float32), gathered, precision=lax.Precision.HIGHEST
    )
    return summed / counts.astype(jnp.float32)[:, None]


def arrange_owned(partial_sum, building_count, case_count):
    wave_size = lax.axis_size("wave")
    dof_size = lax.axis_size("dof")
    arranged = partial_sum.reshape(
        dof_size, building_count // dof_size, wave_size, case_count // wave_size
    )
    arranged = jnp.transpose(arranged, (2, 0, 1, 3))
    return arranged.reshape(wave_size * building_count, case_count // wave_size)


def body(green, rough, axle_pos, axle_load, rows, counts, coupling):
    wave_count = green.shape[1]
    case_count = axle_pos.shape[0]
    building_count = rows.shape[0]
    slot_count = rows.shape[1]
    waves = lax.axis_index("wave") * wave_count + jnp.arange(wave_count, dtype=jnp.int32)
    product = waves[:, None, None] * axle_pos[None, :, :] % K
    angle = product.astype(jnp.float32) * (2.0 * math.pi / K)
    norm_axle = 1.0 / math.sqrt(axle_pos.shape[1])
    phase_re = jnp.sum(axle_load[None] * jnp.cos(angle), axis=2) * norm_axle
    phase_im = -jnp.sum(axle_load[None] * jnp.sin(angle), axis=2) * norm_axle
    force_re = (
        rough[0][:, :, None] * phase_re[:, None, :] - rough[1][:, :, None] * phase_im[:, None, :]
    )
    force_im = (
        rough[0][:, :, None] * phase_im[:, None, :] + rough[1][:, :, None] * phase_re[:, None, :]
    )
    force = jnp.concatenate([force_re, force_im], axis=2).astype(jnp.bfloat16)
    prod_real = jnp.einsum("mji,mjc->mic", green[0], force, preferred_element_type=jnp.float32)
    prod_imag = jnp.einsum("mji,mjc->mic", green[1], force, preferred_element_type=jnp.float32)
    spec_re = prod_real[:, :, :case_count] - prod_imag[:, :, case_count:]
    spec_im = prod_real[:, :, case_count:] + prod_imag[:, :, :case_count]
    spectra = jnp.stack([spec_re, spec_im], axis=1).astype(jnp.bfloat16)
    slots = (jnp.arange(slot_count, dtype=jnp.int32)[None, :] < counts[:, None]).astype(jnp.float32)
    building_ids = jnp.broadcast_to(
        jnp.arange(building_count, dtype=jnp.int32)[:, None], (building_count, slot_count)
    )
    occupancy = (
        jnp.zeros((building_count, K), jnp.float32)
        .at[building_ids, rows]
        .add(slots)
        .astype(jnp.bfloat16)
    )
    table = make_table()
    group_in = lax.all_to_all(spectra, "wave", split_axis=2, concat_axis=0, tiled=True)
    first_len = group_in.shape[2]
    second_len = group_in.shape[3]
    flat = group_in.reshape(group_in.shape[0] * 2, first_len * second_len)
    field = jnp.dot(table, flat, preferred_element_type=jnp.float32)
    field = field.reshape(table.shape[0], first_len, second_len)
    dof_sub = field.shape[1]
    coupling_part = lax.dynamic_slice_in_dim(coupling, lax.axis_index("wave") * dof_sub, dof_sub, 1)
    partial_sum = building_terms(field, coupling_part, occupancy, counts)
    arranged = arrange_owned(partial_sum, building_count, case_count)
    return lax.psum_scatter(arranged, ("wave", "dof"), scatter_dimension=0, tiled=True)


def solution(mesh):
    in_specs = (
        P(None, "wave", None, "dof"),
        P(None, "wave", None),
        P(),
        P(),
        P(),
        P(),
        P(None, "dof"),
    )
    out_specs = P("dof", "wave")
    return jax.shard_map(body, mesh=mesh, in_specs=in_specs, out_specs=out_specs, check_vma=False)
```

profile of v0, /device:TPU:0, one launch (start us, length us, event | category | flops | bytes accessed | tf_op | source)
XLA Modules:
  0.0 811.6 jit_solution(3772090836519859999)
XLA Ops:
  6.5 1.3 slice_bitcast_fusion.1
  7.9 19.9 %multiply_reduce_fusion.1 = (f32[256,128]{1,0:T(8,128)S(1)}, f32[256,128]{1,0:T(8,128)S(1)}) fusion(s32[128,32]{0,1:T(8,128)} %param.9, s32[256]{0:T(256)S(1)} %iota_add_fusion, f32[128,32]{0,1:T(8,128)} %param.10), kind=kLoop, calls=%fused_computation.45 | loop fusion | flops 18808832 | bytes 295936 | tf_op jit(solution)/shard_map/reduce_sum | solution.py:54
  27.8 22.0 %subtract_convert_fusion = (bf16[256,512,128]{1,2,0:T(8,128)(2,1)}, bf16[256,512,128]{1,2,0:T(8,128)(2,1)}) fusion(f32[256,128]{1,0:T(8,128)S(1)} %get-tuple-element.15, f32[256,512]{1,0:T(8,128)S(1)} %get-tuple-element.12, f32[256,128]{1,0:T(8,128)S(1)} %get-tuple-element.16, f32[256,512]{1,0:T(8,128)S(1)} %get-tuple-element.11), kind=kLoop, calls=%fused_computation.3 | loop fusion | flops 134217728 | bytes 68419584 | tf_op jit(solution)/shard_map/convert.4
  49.8 44.8 %fusion.17 = f32[256,128,256]{1,2,0:T(8,128)} fusion(bf16[2,256,512,128]{3,2,1,0:T(8,128)(2,1)} %param.7, bf16[256,512,128]{1,2,0:T(8,128)(2,1)} %get-tuple-element.10, bf16[256,512,128]{1,2,0:T(8,128)(2,1)} %get-tuple-element.9), kind=kOutput, calls=%fused_computation.30 | convolution fusion | flops 8724152320 | bytes 134217728 | tf_op jit(solution)/shard_map/mji,mjc->mic/dot_general | solution.py:63
  94.6 44.8 %fusion.20 = f32[256,128,256]{1,2,0:T(8,128)} fusion(bf16[2,256,512,128]{3,2,1,0:T(8,128)(2,1)} %param.7, bf16[256,512,128]{1,2,0:T(8,128)(2,1)} %get-tuple-element.10, bf16[256,512,128]{1,2,0:T(8,128)(2,1)} %get-tuple-element.9), kind=kOutput, calls=%fused_computation.31 | convolution fusion | flops 8724152320 | bytes 134217728 | tf_op jit(solution)/shard_map/mji,mjc->mic/dot_general | solution.py:64
  139.4 25.9 %fusion.23 = (bf16[256,1,128,128]{2,3,0,1:T(8,128)(2,1)S(1)}, bf16[256,1,128,128]{2,3,0,1:T(8,128)(2,1)}) fusion(f32[256,128,256]{1,2,0:T(8,128)} %fusion.20, f32[256,128,256]{1,2,0:T(8,128)} %fusion.17), kind=kLoop, calls=%fused_computation.32 | loop fusion | flops 16777216 | bytes 83886080 | tf_op jit(solution)/shard_map/stack | solution.py:67
  165.3 10.5 %pad_maximum_fusion.4 = bf16[256,2,128,128]{2,3,0,1:T(8,128)(2,1)} fusion(bf16[256,1,128,128]{2,3,0,1:T(8,128)(2,1)} %get-tuple-element.8, bf16[256,1,128,128]{2,3,0,1:T(8,128)(2,1)S(1)} %get-tuple-element.7), kind=kLoop, calls=%fused_computation.24 | loop fusion | flops 8388608 | bytes 33554432 | tf_op jit(solution)/shard_map/stack | solution.py:67
  175.8 21.7 %copy.33 = bf16[256,2,128,128]{3,0,1,2:T(8,128)(2,1)} copy(bf16[256,2,128,128]{2,3,0,1:T(8,128)(2,1)} %pad_maximum_fusion.4) | data formatting | bytes 33554432 | tf_op jit(solution)/shard_map/stack | solution.py:67
  197.5 7.3 all-to-all-start
  204.8 0.4 reduce-scatter.2.cloned.1.call-start
  205.2 67.7 %multiply_convert_fusion = (bf16[2048,2048,1]{1,0,2:T(8,128)(2,1)S(1)}, bf16[2048,2048,1]{1,0,2:T(8,128)(2,1)S(1)}) fusion(), kind=kLoop, calls=%fused_computation.25 | loop fusion | flops 79691776 | bytes 16777216 | tf_op jit(solution)/shard_map/convert.7
  272.9 6.8 pad_maximum_fusion.3
  279.7 41.6 %copy.32 = bf16[2048,2048,2]{0,2,1:T(2,128)(2,1)} copy(bf16[2048,2048,2]{1,0,2:T(8,128)(2,1)} %pad_maximum_fusion.3) | data formatting | bytes 33554432 | tf_op jit(solution)/shard_map/stack | solution.py:16
  321.3 24.9 %convert_element_type.45 = bf16[2048,4096]{0,1:T(8,128)(2,1)} reshape(bf16[2048,2048,2]{0,2,1:T(2,128)(2,1)} %copy.32) | data formatting | bytes 33554432 | tf_op jit(solution)/shard_map/convert_element_type | solution.py:17
  346.4 0.2 copy.31
  346.6 0.2 reshape.136
  346.8 0.2 fusion.32
  347.1 0.2 reshape.138
  347.3 89.8 %scatter_custom_fusion = f32[2097152]{0:T(1024)} fusion(s32[16384]{0:T(1024)S(1)} %reshape.136, f32[16384]{0:T(1024)S(1)} %reshape.138, f32[]{:T(128)} %constant.24.clone.1), kind=kCustom, calls=%fused_computation.42 | custom fusion | flops 16384 | bytes 8388612
  437.1 5.1 convert_element_type.48
  442.1 7.3 reshape.135
  449.5 0.1 dynamic-slice_bitcast_fusion
  449.6 118.3 %all-to-all-done = bf16[256,2,128,128]{3,0,1,2:T(8,128)(2,1)} async-done(((bf16[256,2,128,128]{3,0,1,2:T(8,128)(2,1)}), bf16[256,2,128,128]{3,0,1,2:T(8,128)(2,1)}, u32[]{:S(2)}, u32[]{:S(2)}) %all-to-all-start) | async-done | bytes 16777248 | tf_op jit(solution)/shard_map/all_to_all | solution.py:79
  567.9 18.5 %copy.35 = bf16[8,256,2,16,128]{4,3,2,1,0:T(8,128)(2,1)} copy(bf16[8,256,2,16,128]{4,1,2,3,0:T(8,128)(2,1)} %bitcast.12) | data formatting | bytes 33554432 | tf_op jit(solution)/shard_map/all_to_all | solution.py:79
  586.4 43.6 %fusion.9 = f32[2048,2048]{1,0:T(8,128)} fusion(bf16[2048,4096]{0,1:T(8,128)(2,1)} %convert_element_type.45, bf16[512,8,16,128]{3,2,1,0:T(8,128)(2,1)} %bitcast.61), kind=kOutput, calls=%fused_computation.16 | convolution fusion | flops 34359738368 | bytes 50331648 | tf_op jit(solution)/shard_map/dot_general | solution.py:83
  630.0 30.8 %convolution_bitcast_fusion = f32[128,8,16,128]{3,1,2,0:T(8,128)S(1)} fusion(bf16[1024,2048]{1,0:T(8,128)(2,1)} %reshape.135, f32[2048,2048]{1,0:T(8,128)} %fusion.9), kind=kOutput, calls=%fused_computation.46 | convolution fusion | flops 51539607552 | bytes 29360128 | tf_op jit(solution)/shard_map/dot_general | solution.py:22
  660.8 2.0 copy.41
  662.8 6.7 fusion.30
  669.6 0.3 copy.38
  670.0 0.2 reshape.129
  670.3 1.1 reshape.130
  671.4 133.2 %reduce-scatter.2.cloned.1.call-done = f32[256,16]{0,1:T(8,128)} async-done(((f32[8192,16]{0,1:T(8,128)}), f32[256,16]{0,1:T(8,128)}) %reduce-scatter.2.cloned.1.call-update) | async-done | bytes 16400 | tf_op jit(solution)/shard_map/reduce_scatter | solution.py:89
  (21 shorter events, 0.4 us)
Async XLA Ops:
  6.5 442.9 %copy-start = (bf16[1024,128]{1,0:T(8,128)(2,1)S(1)}, bf16[1024,128]{1,0:T(8,128)(2,1)}, u32[]{:S(2)}) copy-start(bf16[1024,128]{1,0:T(8,128)(2,1)} %param.13) | copy-start | bytes 786436
  197.5 370.4 %all-to-all-start = ((bf16[256,2,128,128]{3,0,1,2:T(8,128)(2,1)}), bf16[256,2,128,128]{3,0,1,2:T(8,128)(2,1)}, u32[]{:S(2)}, u32[]{:S(2)}) async-start(bf16[256,2,128,128]{3,0,1,2:T(8,128)(2,1)} %copy.33), calls=%async_computation | async-start | bytes 33554432 | tf_op jit(solution)/shard_map/all_to_all | solution.py:79
  204.8 599.8 %reduce-scatter.2.cloned.1.call-start = ((), (), s32[]{:S(2)}) async-start(), calls=%async_computation.2 | async-start | bytes 540672 | tf_op jit(solution)/shard_map/reduce_scatter | solution.py:89
  321.3 24.9 %copy-start.1 = (s32[1024,16]{0,1:T(8,128)S(1)}, s32[1024,16]{0,1:T(8,128)}, u32[]{:S(2)}) copy-start(s32[1024,16]{0,1:T(8,128)} %param.11) | copy-start | bytes 196612
  321.3 24.9 %copy-start.4 = (s32[2]{0:T(128)S(1)}, s32[2]{0:T(128)}, u32[]{:S(2)}) copy-start(s32[2]{0:T(128)} %constant.50) | copy-start | bytes 28
  321.3 25.0 %copy-start.3 = (s32[2]{0:T(128)S(1)}, s32[2]{0:T(128)}, u32[]{:S(2)}) copy-start(s32[2]{0:T(128)} %constant.53) | copy-start | bytes 28
  321.3 25.6 %copy-start.2 = (s32[1024]{0:T(1024)S(1)}, s32[1024]{0:T(1024)}, u32[]{:S(2)}) copy-start(s32[1024]{0:T(1024)} %param.12) | copy-start | bytes 12292
Sparse Core Ops, SparseCore 0:
  671.5 133.0 reduce-scatter.1
where the time goes:
time: 823 us; the launch traced here: 812 us
  waiting for transfers between devices  251 us (30%)
  other arithmetic  248 us (30%)
  matrix products  171 us (21%)
  local copies, waits for them, and re-layouts  120 us (15%)
  between operations  13.8 us (2%)
    reduce_scatter x1, waiting for transfers between devices, body(): lax.psum_scatter(arranged, ('wave', 'dof'), scatter_dimension=0, tiled=True)  133 us
    all_to_all x1, waiting for transfers between devices, body(): lax.all_to_all(spectra, 'wave', split_axis=2, concat_axis=0, tiled=True)  118 us
    unnamed x4, other arithmetic  90 us
    another operation x2, other arithmetic  89.7 us
    dot_general x1, matrix products, body(): jnp.einsum('mji,mjc->mic', green[0], force, preferred_element_type=jnp.fl...  44.8 us
    dot_general x1, matrix products, body(): jnp.einsum('mji,mjc->mic', green[1], force, preferred_element_type=jnp.fl...  44.8 us
    dot_general x1, matrix products, body(): field = jnp.dot(table, flat, preferred_element_type=jnp.float32)  43.6 us
    another operation x1, local copies, waits for them, and re-layouts, make_table(): table = jnp.stack([jnp.cos(angle) * scale, -jnp.sin(angle) * scale], axis=2)  41.6 us
  transfers between devices with their start and end apart: 2, of which 2 were waited for; matrix products, arithmetic and copies ran while one was open for 30% of the time, Pallas kernels for 0%

commit v1 on v0

v1 whole, which is shorter than its diff:
```python
import functools
import math

import jax
import jax.numpy as jnp
import numpy as np
from jax import lax
from jax.experimental import pallas as pl
from jax.experimental.pallas import tpu as pltpu
from jax.sharding import PartitionSpec as P

K = 2048
LOW = 128
HIGH = K // LOW
GROUP = 256
STEP = 8
SLOTS = 16

F32 = jnp.float32
BF16 = jnp.bfloat16


def dot_nn(a, b):
    return lax.dot_general(a, b, (((1,), (0,)), ((), ())), preferred_element_type=F32)


def dot_nt(a, b):
    return lax.dot_general(a, b, (((1,), (1,)), ((), ())), preferred_element_type=F32)


def split(x):
    hi = x.astype(BF16)
    return hi, (x - hi.astype(F32)).astype(BF16)


def iota(shape, axis):
    return lax.broadcasted_iota(jnp.int32, shape, axis)


def wave_block(wave_count):
    return min(128, wave_count)


def factor_tables(wave_size, wave_count):
    block = wave_block(wave_count)

    def one(stations, scale):
        waves = np.arange(wave_size * wave_count).reshape(wave_size, 1, wave_count // block, block)
        angle = (waves * stations[None, :, None, None] % K) * (2.0 * np.pi / K)
        both = np.stack([np.cos(angle), -np.sin(angle)], axis=3) * scale
        return both.reshape(wave_size, len(stations), 2 * wave_count).astype(np.float32)

    return one(np.arange(LOW), 1.0 / math.sqrt(K)), one(np.arange(HIGH) * LOW, 1.0)[:, :, None]


def one_hot_rows(key, weights):
    parts = [jnp.where(key == float(h), w, 0.0) for w in weights for h in range(HIGH)]
    return jnp.concatenate(parts, axis=0).astype(BF16)


def spread(values, per_item):
    items = GROUP // per_item
    shape = (values.shape[0], GROUP)
    own = iota(shape, 1) // per_item == iota(shape, 0) % items
    copies = jnp.where(
        iota((per_item, GROUP), 1) % per_item == iota((per_item, GROUP), 0), 1.0, 0.0
    ).astype(BF16)
    return dot_nn(values.astype(BF16), copies), own


def kernel(
    sizes,
    green,
    rough,
    axle_pos,
    axle_load,
    rows,
    counts,
    coupling,
    low_table,
    high_table,
    out,
    ring,
    rough_v,
    pos_v,
    load_v,
    rows_v,
    counts_v,
    coupling_v,
    low_v,
    high_v,
    table_hi,
    table_lo,
    key_v,
    low_key_v,
    occupancy,
    weights_v,
    loads,
    phase_v,
    g_v,
    total,
    small_sem,
    ring_sem,
):
    wave_size, dof_size = sizes
    wave_count, _, resp = green.shape[1:]
    slot_count, building_count = rows.shape
    axle_count, case_count = axle_pos.shape
    block = wave_block(wave_count)
    blocks = wave_count // block
    steps = wave_count // STEP
    wave = lax.axis_index("wave")

    small = [
        pltpu.make_async_copy(src, dst, small_sem.at[i])
        for i, (src, dst) in enumerate(
            [
                (low_table.at[wave], low_v),
                (high_table.at[wave], high_v),
                (rows, rows_v),
                (counts, counts_v),
                (axle_pos, pos_v),
                (axle_load, load_v),
                (coupling, coupling_v),
                (rough, rough_v),
            ]
        )
    ]
    for copy in small:
        copy.start()

    def green_copy(step, slot):
        return pltpu.make_async_copy(
            green.at[:, pl.ds(step * STEP, STEP)], ring.at[slot], ring_sem.at[slot]
        )

    held = min(SLOTS, steps)
    for step in range(held):
        green_copy(step, step).start()
    for copy in small:
        copy.wait()

    @pl.loop(0, HIGH)
    def _(h):
        at = pl.ds(pl.multiple_of(h * LOW, LOW), LOW)
        for q in range(blocks):
            re = slice(2 * q * block, (2 * q + 1) * block)
            im = slice((2 * q + 1) * block, (2 * q + 2) * block)
            low_re, low_im = low_v[:, re], low_v[:, im]
            high_re, high_im = high_v[h, :, re], high_v[h, :, im]
            table_hi[at, re], table_lo[at, re] = split(low_re * high_re - low_im * high_im)
            table_hi[at, im], table_lo[at, im] = split(low_re * high_im + low_im * high_re)

    for k in range(building_count // 128):
        at = slice(128 * k, 128 * (k + 1))
        x = rows_v[:, at]
        valid = iota((slot_count, 128), 0) < counts_v[k : k + 1, :]
        high, own = spread(jnp.where(valid, x // LOW, -1).astype(F32).T, slot_count)
        low, _ = spread((x % LOW).astype(F32).T, slot_count)
        key_v[at, :] = jnp.where(own, high, -1.0)
        low_key_v[at, :] = jnp.where(own, low, 0.0)

    def low_rows(low):
        row = jnp.sum(low, axis=0, keepdims=True)
        return jnp.where(row == iota((LOW, GROUP), 0).astype(F32), 1.0, 0.0).astype(BF16)

    items = GROUP // slot_count

    @pl.loop(0, building_count // items, unroll=4)
    def _(g):
        at = pl.ds(pl.multiple_of(g * items, items), items)
        found = dot_nt(one_hot_rows(key_v[at, :], [1.0]), low_rows(low_key_v[at, :]))
        for h in range(HIGH):
            occupancy[at, h * LOW : (h + 1) * LOW] = found[h * items : (h + 1) * items].astype(BF16)

    @pl.loop(0, building_count // 256)
    def _(r):
        at = pl.ds(pl.multiple_of(r * 256, 256), 256)
        weights_v[at, :] = dot_nn(occupancy[at, :], table_hi[...])

    x = pos_v[...]
    high, own = spread((x // LOW).astype(F32).T, axle_count)
    low, _ = spread((x % LOW).astype(F32).T, axle_count)
    high, low = jnp.where(own, high, -1.0), jnp.where(own, low, 0.0)
    load_parts = [spread(part.astype(F32), axle_count)[0] for part in split(load_v[...].T)]
    items_c = GROUP // axle_count
    for g in range(case_count // items_c):
        at = slice(g * items_c, (g + 1) * items_c)
        found = dot_nt(
            one_hot_rows(high[at], [part[at] for part in load_parts]), low_rows(low[at])
        )
        found = found[: HIGH * items_c] + found[HIGH * items_c :]
        for h in range(HIGH):
            loads[at, h * LOW : (h + 1) * LOW] = found[h * items_c : (h + 1) * items_c]
    load_hi, load_lo = split(loads[...])
    phase = (
        dot_nn(load_hi, table_hi[...]) + dot_nn(load_lo, table_hi[...]) + dot_nn(load_hi, table_lo[...])
    ) * math.sqrt(K / axle_count)
    phase_hi, phase_lo = split(phase)
    phase_v[:case_count, :] = phase_hi
    phase_v[case_count:, :] = phase_lo

    def one_step(step, block_start):
        slot = lax.rem(step, held)
        green_copy(step, slot).wait()
        at = pl.ds(pl.multiple_of(step * STEP, STEP), STEP)
        re_hi, re_lo = split(rough_v[0, at, :])
        im_hi, im_lo = split(rough_v[1, at, :])
        left = jnp.concatenate(
            [
                jnp.concatenate([a.astype(F32), b.astype(F32)], axis=1)
                for a, b in ((re_hi, -im_hi), (im_hi, re_hi), (re_lo, -im_lo), (im_lo, re_lo))
            ],
            axis=0,
        ).astype(BF16)
        rank = iota((STEP, resp), 0)
        g_re = jnp.zeros((STEP, resp), F32)
        g_im = jnp.zeros((STEP, resp), F32)
        for k in range(STEP):
            right = jnp.concatenate([ring[slot, 0, k], ring[slot, 1, k]], axis=0)
            prod = dot_nn(left, right)
            g_re = jnp.where(rank == k, prod[:STEP] + prod[2 * STEP : 3 * STEP], g_re)
            g_im = jnp.where(rank == k, prod[STEP : 2 * STEP] + prod[3 * STEP :], g_im)
        row = step * STEP - block_start
        g_v[pl.ds(pl.multiple_of(row, STEP), STEP), :] = g_re
        g_v[pl.ds(pl.multiple_of(block + row, STEP), STEP), :] = g_im

        @pl.when(step + held < steps)
        def _():
            green_copy(step + held, slot).start()

    owned_cases = case_count // wave_size
    owned_buildings = building_count // dof_size
    per_tile = owned_buildings // 128
    for q in range(blocks):

        @pl.loop(q * block // STEP, (q + 1) * block // STEP)
        def _(step):
            one_step(step, q * block)

        g_both = jnp.concatenate(split(g_v[...]), axis=1)
        re = slice(2 * q * block, (2 * q + 1) * block)
        im = slice((2 * q + 1) * block, (2 * q + 2) * block)
        phase_q = phase_v[:, 2 * q * block : (2 * q + 2) * block]
        for d in range(dof_size):
            at = slice(d * owned_buildings, (d + 1) * owned_buildings)
            coupling_d = coupling_v[at, :]
            h = dot_nt(jnp.concatenate([coupling_d, coupling_d], axis=1), g_both)
            h_re, h_im = h[:, :block], h[:, block:]
            w_re, w_im = weights_v[at, re], weights_v[at, im]
            both = jnp.concatenate([w_re * h_re + w_im * h_im, w_im * h_re - w_re * h_im], axis=1)
            both_hi, both_lo = split(both)
            prod = dot_nt(phase_q, both_hi)
            part = prod[:case_count] + prod[case_count:] + dot_nt(phase_q[:case_count], both_lo)
            if q:
                part = part + total[:, at]
            if q < blocks - 1:
                total[:, at] = part
                continue
            count = jnp.concatenate(
                [counts_v[d * per_tile + t : d * per_tile + t + 1, :] for t in range(per_tile)], axis=1
            )
            part = part / count.astype(F32)
            for w in range(wave_size):
                out[w * dof_size + d] = part[w * owned_cases : (w + 1) * owned_cases].astype(BF16)


def body(green, rough, axle_pos, axle_load, rows, counts, coupling):
    wave_size = lax.axis_size("wave")
    dof_size = lax.axis_size("dof")
    wave_count, force_count, resp = green.shape[1:]
    building_count, slot_count = rows.shape
    case_count, axle_count = axle_pos.shape
    low_table, high_table = factor_tables(wave_size, wave_count)
    held = min(SLOTS, wave_count // STEP)
    owned = (case_count // wave_size, building_count // dof_size)
    any_spec = pl.BlockSpec(memory_space=pl.ANY)
    partial_sum = pl.pallas_call(
        functools.partial(kernel, (wave_size, dof_size)),
        out_shape=jax.ShapeDtypeStruct((wave_size * dof_size, *owned), BF16),
        in_specs=[any_spec] * 9,
        out_specs=pl.BlockSpec(memory_space=pltpu.VMEM),
        scratch_shapes=[
            pltpu.VMEM((held, 2, STEP, force_count, resp), BF16),
            pltpu.VMEM(rough.shape, F32),
            pltpu.VMEM((axle_count, case_count), jnp.int32),
            pltpu.VMEM((axle_count, case_count), F32),
            pltpu.VMEM((slot_count, building_count), jnp.int32),
            pltpu.VMEM((building_count // 128, 128), jnp.int32),
            pltpu.VMEM(coupling.shape, BF16),
            pltpu.VMEM(low_table.shape[1:], F32),
            pltpu.VMEM(high_table.shape[1:], F32),
            pltpu.VMEM((K, 2 * wave_count), BF16),
            pltpu.VMEM((K, 2 * wave_count), BF16),
            pltpu.VMEM((building_count, GROUP), F32),
            pltpu.VMEM((building_count, GROUP), F32),
            pltpu.VMEM((building_count, K), BF16),
            pltpu.VMEM((building_count, 2 * wave_count), F32),
            pltpu.VMEM((case_count, K), F32),
            pltpu.VMEM((2 * case_count, 2 * wave_count), BF16),
            pltpu.VMEM((2 * wave_block(wave_count), resp), F32),
            pltpu.VMEM((case_count, building_count), F32),
            pltpu.SemaphoreType.DMA((8,)),
            pltpu.SemaphoreType.DMA((held,)),
        ],
        compiler_params=pltpu.CompilerParams(vmem_limit_bytes=60 * 1024 * 1024),
    )(
        green,
        rough,
        axle_pos.T,
        axle_load.T,
        rows.T,
        counts.reshape(building_count // 128, 128),
        coupling,
        jnp.asarray(low_table),
        jnp.asarray(high_table),
    )
    arrived = lax.all_to_all(partial_sum, ("wave", "dof"), 0, 0)
    return jnp.sum(arrived.astype(F32), axis=0).T


def solution(mesh):
    in_specs = (
        P(None, "wave", None, "dof"),
        P(None, "wave", None),
        P(),
        P(),
        P(),
        P(),
        P(None, "dof"),
    )
    out_specs = P("dof", "wave")
    return jax.shard_map(body, mesh=mesh, in_specs=in_specs, out_specs=out_specs, check_vma=False)
```

time: 823 us -> 56.6 us (0.07); the launches traced: 812 us -> 56.4 us
  waiting for transfers between devices: 251 us -> 0 us
  other arithmetic: 248 us -> 0.65 us
  matrix products: 171 us -> 0 us
  local copies, waits for them, and re-layouts: 120 us -> 0 us
  Pallas kernels: 0 us -> 37.8 us
  blocking collectives: 0 us -> 17.9 us
  between operations: 13.8 us -> 0.01 us
    dot_general x5 -> x0, matrix products: 171 us -> none  [the longest x1 44.8 us: body(): jnp.einsum('mji,mjc->mic', green[0], force, preferred_element_type=jnp.fl...]
    reduce_scatter x1 -> x0, waiting for transfers between devices: 133 us -> none  [body(): lax.psum_scatter(arranged, ('wave', 'dof'), scatter_dimension=0, tiled=True)]
    another operation x5 -> x0, other arithmetic: 133 us -> none
    all_to_all x1 -> x0, waiting for transfers between devices: 118 us -> none  [body(): lax.all_to_all(spectra, 'wave', split_axis=2, concat_axis=0, tiled=True)]
    unnamed x4 -> x0, other arithmetic: 90 us -> none
    another operation x2 -> x0, local copies, waits for them, and re-layouts: 63.3 us -> none  [the longest x1 41.6 us: make_table(): table = jnp.stack([jnp.cos(angle) * scale, -jnp.sin(angle) * scale], axis=2)]
    pallas_call x0 -> x1, Pallas kernels: none -> 37.8 us  [body(): pl.pallas_call(functools.partial(kernel, (wave_size, dof_size)), out_shap...]
    convert_element_type x3 -> x0, local copies, waits for them, and re-layouts: 32.4 us -> none  [the longest x1 24.9 us: make_table(): return table.reshape(K, 2 * K).astype(jnp.bfloat16)]
  transfers between devices with their start and end apart: 2 -> 0, of which waited for: 2 -> 0; matrix products, arithmetic and copies ran while one was open for 30% -> 0% of each run, Pallas kernels for 0% -> 0%
where the time goes in v1:
time: 56.6 us; the launch traced here: 56.4 us
  Pallas kernels  37.8 us (67%)
  blocking collectives  17.9 us (32%)
  other arithmetic  0.65 us (1%)
    pallas_call x1, Pallas kernels, body(): pl.pallas_call(functools.partial(kernel, (wave_size, dof_size)), out_shap...  37.8 us
    all_to_all x1, blocking collectives, body(): arrived = lax.all_to_all(partial_sum, ('wave', 'dof'), 0, 0)  17.9 us

profile of v1, /device:TPU:0, one launch (start us, length us, event | category | flops | bytes accessed | tf_op | source)
XLA Modules:
  0.0 56.4 jit_solution(8168722073381821915)
XLA Ops:
  0.0 37.8 %shard_map.91 = bf16[32,16,256]{2,1,0:T(8,128)(2,1)} custom-call(bf16[2,256,512,128]{3,2,1,0:T(8,128)(2,1)} %green.1, f32[2,256,512]{2,1,0:T(8,128)} %rough.1, s32[32,128]{1,0:T(8,128)} %bitcast.6, f32[32,128]{1,0:T(8,128)} %bitcast.7, s32[16,1024]{1,0:T(8,128)} %bitcast.5, s32[8,128]{1,0:T(8,128)} %bitcast.8, bf16[1024,128]{1,0:T(8,128)(2,1)} %coupling.1, ...), custom_call_target="tpu_custom_call" | custom-call | tf_op jit(solution)/shard_map/pallas_call | solution.py:278
  37.8 17.9 %all_to_all.5 = bf16[32,16,256]{2,1,0:T(8,128)(2,1)S(1)} all-to-all(bf16[32,16,256]{2,1,0:T(8,128)(2,1)} %shard_map.91), channel_id=1, replica_groups=mesh['wave'=8,'dof'=4] {'wave','dof'}, dimensions={0} | all-to-all | bytes 524288 | tf_op jit(solution)/shard_map/all_to_all | solution.py:318
  55.7 0.7 %convert_reduce_fusion = f32[16,256]{1,0:T(8,128)} fusion(bf16[32,16,256]{2,1,0:T(8,128)(2,1)S(1)} %all_to_all.5), kind=kLoop, calls=%fused_computation | loop fusion | flops 258048 | bytes 278528 | tf_op jit(solution)/shard_map/reduce_sum | solution.py:319

commit v2 on v1

v2 whole, which is shorter than its diff:
```python
import functools
import math

import jax
import jax.numpy as jnp
import numpy as np
from jax import lax
from jax.experimental import pallas as pl
from jax.experimental.pallas import tpu as pltpu
from jax.sharding import PartitionSpec as P

K = 2048
HALF = K // 2
LOW = 128
HIGH = HALF // LOW
GROUP = 256
STEP = 8
AHEAD = 4

F32 = jnp.float32
BF16 = jnp.bfloat16


def dot_nn(a, b):
    return lax.dot_general(a, b, (((1,), (0,)), ((), ())), preferred_element_type=F32)


def dot_nt(a, b):
    return lax.dot_general(a, b, (((1,), (1,)), ((), ())), preferred_element_type=F32)


def split(x):
    hi = x.astype(BF16)
    return hi, (x - hi.astype(F32)).astype(BF16)


def iota(shape, axis):
    return lax.broadcasted_iota(jnp.int32, shape, axis)


def factor_tables(wave_size, wave_count):
    block = wave_count // 2

    def one(stations, scale):
        waves = np.arange(wave_size * wave_count).reshape(wave_size, 1, block, 2)
        waves = np.moveaxis(waves, 3, 2)
        angle = (waves * stations[None, :, None, None] % K) * (2.0 * np.pi / K)
        both = np.stack([np.cos(angle), -np.sin(angle)], axis=3) * scale
        return both.reshape(wave_size, len(stations), 2 * wave_count).astype(np.float32)

    return one(np.arange(LOW), 1.0 / math.sqrt(K)), one(np.arange(HIGH) * LOW, 1.0)


def one_hot_rows(key, weights, dtype):
    zero = jnp.zeros(key.shape, dtype)
    parts = [
        jnp.where(key == jnp.full(key.shape, h, dtype), w, zero) for w in weights for h in range(HIGH)
    ]
    return jnp.concatenate(parts, axis=0)


def low_rows(row, dtype):
    shape = (LOW, GROUP)
    hit = iota(shape, 0).astype(F32).astype(dtype) == jnp.broadcast_to(row, shape)
    return jnp.where(hit, jnp.ones(shape, dtype), jnp.zeros(shape, dtype))


def spread(values, per_item):
    copies = jnp.where(
        iota((per_item, GROUP), 1) % per_item == iota((per_item, GROUP), 0), 1.0, 0.0
    ).astype(BF16)
    shape = (values.shape[0], GROUP)
    own = iota(shape, 1) // per_item == iota(shape, 0) % (GROUP // per_item)
    return jnp.where(own, dot_nn(values.astype(BF16), copies), 0.0)


def station_parts(x):
    top = x >= HALF
    sign = jnp.where(top, -1.0, 1.0)
    high = lax.shift_right_logical(x, LOW.bit_length() - 1) & (HIGH - 1)
    return sign, (high + 1).astype(F32), (x & (LOW - 1)).astype(F32)


def kernel(
    sizes,
    green,
    rough,
    axle_pos,
    axle_load,
    rows,
    counts,
    coupling,
    low_table,
    high_table,
    out,
    ring,
    rough_v,
    pos_v,
    load_v,
    rows_v,
    counts_v,
    coupling_v,
    low_v,
    high_v,
    table_hi,
    table_lo,
    key_v,
    sign_v,
    low_key_v,
    occupancy,
    weights_v,
    loads,
    phase_v,
    g_v,
    total,
    small_sem,
    ring_sem,
):
    wave_size, dof_size = sizes
    block, _, _, resp = green.shape[1:]
    slot_count, building_count = rows.shape
    axle_count, case_count = axle_pos.shape
    steps = 2 * block // STEP
    held = steps // 2
    slots = ring.shape[0]
    wave = lax.axis_index("wave")

    small = [
        pltpu.make_async_copy(src, dst, small_sem.at[i])
        for i, (src, dst) in enumerate(
            [
                (rows, rows_v),
                (counts, counts_v),
                (low_table.at[wave], low_v),
                (high_table.at[wave], high_v),
                (axle_pos, pos_v),
                (axle_load, load_v),
                (coupling, coupling_v),
            ]
            + [
                (rough.at[:, :, t * 128 : (t + 1) * 128], rough_v.at[t])
                for t in range(rough_v.shape[0])
            ]
        )
    ]
    for copy in small:
        copy.start()

    def green_copy(step):
        slot = lax.rem(step, slots)
        per_block = steps // 2
        at = pl.ds(lax.rem(step, per_block) * STEP, STEP)
        return pltpu.make_async_copy(
            green.at[:, at, step // per_block], ring.at[slot], ring_sem.at[slot]
        )

    for step in range(held):
        green_copy(jnp.int32(step)).start()
    for copy in small[:2]:
        copy.wait()

    items = GROUP // slot_count
    for k in range(building_count // 128):
        at = slice(128 * k, 128 * (k + 1))
        sign, high, low = station_parts(rows_v[:, at])
        used = iota((slot_count, 128), 0) < counts_v[k : k + 1, :]
        key_v[at, :] = spread(jnp.where(used, high, 0.0).T, slot_count).astype(BF16)
        sign_v[at, :] = spread(sign.T, slot_count).astype(BF16)
        groups = 128 // items
        member = jnp.where(iota((groups, 128), 1) // items == iota((groups, 128), 0), 1.0, 0.0)
        low_key_v[groups * k : groups * (k + 1), :] = dot_nn(
            member.astype(BF16), spread(low.T, slot_count).astype(BF16)
        )

    @pl.loop(0, building_count // (8 * items))
    def _(r):
        low_eight = low_key_v[pl.ds(pl.multiple_of(r * 8, 8), 8), :]
        for k in range(8):
            at = pl.ds(pl.multiple_of((r * 8 + k) * items, items), items)
            key = key_v[at, :] - jnp.ones((items, GROUP), BF16)
            hot = one_hot_rows(key, [jnp.ones((items, GROUP), BF16), sign_v[at, :]], BF16)
            low = low_eight[k : k + 1, :].astype(BF16)
            found = dot_nt(hot, low_rows(low, BF16)).astype(BF16)
            for h in range(HIGH):
                for top in range(2):
                    row = (top * HIGH + h) * items
                    occupancy[top, at, h * LOW : (h + 1) * LOW] = found[row : row + items]

    for copy in small[2:6]:
        copy.wait()

    for h in range(HIGH):
        at = slice(h * LOW, (h + 1) * LOW)
        for q in range(2):
            re = slice(2 * q * block, (2 * q + 1) * block)
            im = slice((2 * q + 1) * block, (2 * q + 2) * block)
            low_re, low_im = low_v[:, re], low_v[:, im]
            high_re, high_im = high_v[h : h + 1, re], high_v[h : h + 1, im]
            table_hi[at, re], table_lo[at, re] = split(low_re * high_re - low_im * high_im)
            table_hi[at, im], table_lo[at, im] = split(low_re * high_im + low_im * high_re)

    for step in range(held, held + AHEAD):
        green_copy(jnp.int32(step)).start()

    @pl.loop(0, building_count // 256)
    def _(r):
        at = pl.ds(pl.multiple_of(r * 256, 256), 256)
        for q in range(2):
            cols = slice(2 * q * block, (2 * q + 2) * block)
            weights_v[at, cols] = dot_nn(occupancy[q, at, :], table_hi[:, cols])

    sign, high, low = station_parts(pos_v[...])
    high = spread(high.T, axle_count) - 1.0
    low = spread(low.T, axle_count)
    load_parts = []
    for part in split(load_v[...]):
        load_parts += [part.astype(F32), sign * part.astype(F32)]
    load_parts = [spread(part.T, axle_count) for part in load_parts]
    items_c = GROUP // axle_count
    for g in range(case_count // items_c):
        at = slice(g * items_c, (g + 1) * items_c)
        hot = one_hot_rows(high[at], [part[at] for part in load_parts], F32)
        row = jnp.sum(low[at], axis=0, keepdims=True)
        found = dot_nt(hot.astype(BF16), low_rows(row, F32).astype(BF16))
        found = found[: 2 * HIGH * items_c] + found[2 * HIGH * items_c :]
        for top in range(2):
            for h in range(HIGH):
                row = (top * HIGH + h) * items_c
                loads[top, at, h * LOW : (h + 1) * LOW] = found[row : row + items_c]
    for q in range(2):
        cols = slice(2 * q * block, (2 * q + 2) * block)
        load_hi, load_lo = split(loads[q])
        phase = (
            dot_nn(load_hi, table_hi[:, cols])
            + dot_nn(load_lo, table_hi[:, cols])
            + dot_nn(load_hi, table_lo[:, cols])
        ) * math.sqrt(K / axle_count)
        phase_v[:case_count, cols], phase_v[case_count:, cols] = split(phase)

    for copy in small[6:]:
        copy.wait()

    def pump(step):
        green_copy(step).wait()

        @pl.when(step + AHEAD < steps)
        def _():
            green_copy(step + AHEAD).start()

    def one_step(step, q):
        slot = lax.rem(step, slots)
        row = pl.multiple_of((step - q * (steps // 2)) * STEP, STEP)
        at = pl.ds(2 * row + q, STEP, stride=2)
        rough_re, rough_im = (
            jnp.concatenate([rough_v[t, part, at, :] for t in range(rough_v.shape[0])], axis=1)
            for part in range(2)
        )
        re_hi, re_lo = split(rough_re)
        im_hi, im_lo = split(rough_im)
        left = jnp.concatenate(
            [
                jnp.concatenate([a.astype(F32), b.astype(F32)], axis=1)
                for a, b in ((re_hi, -im_hi), (im_hi, re_hi), (re_lo, -im_lo), (im_lo, re_lo))
            ],
            axis=0,
        ).astype(BF16)
        rank = iota((STEP, resp), 0)
        g_re = jnp.zeros((STEP, resp), F32)
        g_im = jnp.zeros((STEP, resp), F32)
        for k in range(STEP):
            right = jnp.concatenate([ring[slot, 0, k], ring[slot, 1, k]], axis=0)
            prod = dot_nn(left, right)
            g_re = jnp.where(rank == k, prod[:STEP] + prod[2 * STEP : 3 * STEP], g_re)
            g_im = jnp.where(rank == k, prod[STEP : 2 * STEP] + prod[3 * STEP :], g_im)
        g_v[pl.ds(row, STEP), :] = g_re
        g_v[pl.ds(block + row, STEP), :] = g_im

    for step in range(held):
        green_copy(jnp.int32(step)).wait()

    owned_cases = case_count // wave_size
    owned_buildings = building_count // dof_size
    per_tile = owned_buildings // 128
    for q in range(2):

        @pl.loop(q * steps // 8, (q + 1) * steps // 8)
        def _(r):
            for k in range(4):
                if k % 2:
                    pump(held + 2 * r + k // 2)
                one_step(4 * r + k, q)

        g_both = jnp.concatenate(split(g_v[...]), axis=1)
        re = slice(2 * q * block, (2 * q + 1) * block)
        im = slice((2 * q + 1) * block, (2 * q + 2) * block)
        phase_q = phase_v[:, 2 * q * block : (2 * q + 2) * block]
        for d in range(dof_size):
            at = slice(d * owned_buildings, (d + 1) * owned_buildings)
            coupling_d = coupling_v[at, :]
            h = dot_nt(jnp.concatenate([coupling_d, coupling_d], axis=1), g_both)
            h_re, h_im = h[:, :block], h[:, block:]
            w_re, w_im = weights_v[at, re], weights_v[at, im]
            both = jnp.concatenate([w_re * h_re + w_im * h_im, w_im * h_re - w_re * h_im], axis=1)
            both_hi, both_lo = split(both)
            prod = dot_nt(phase_q, both_hi)
            part = prod[:case_count] + prod[case_count:] + dot_nt(phase_q[:case_count], both_lo)
            if q == 0:
                total[:, at] = part
                continue
            count = jnp.concatenate(
                [counts_v[d * per_tile + t : d * per_tile + t + 1, :] for t in range(per_tile)], axis=1
            )
            part = (total[:, at] + part) * (1.0 / count.astype(F32))
            for w in range(wave_size):
                out[w * dof_size + d] = part[w * owned_cases : (w + 1) * owned_cases].astype(BF16)


def body(green, rough, axle_pos, axle_load, rows, counts, coupling):
    wave_size = lax.axis_size("wave")
    dof_size = lax.axis_size("dof")
    _, wave_count, force_count, resp = green.shape
    building_count, slot_count = rows.shape
    case_count, axle_count = axle_pos.shape
    block = wave_count // 2
    low_table, high_table = factor_tables(wave_size, wave_count)
    slots = block // STEP + AHEAD
    owned = (case_count // wave_size, building_count // dof_size)
    any_spec = pl.BlockSpec(memory_space=pl.ANY)
    partial_sum = pl.pallas_call(
        functools.partial(kernel, (wave_size, dof_size)),
        out_shape=jax.ShapeDtypeStruct((wave_size * dof_size, *owned), BF16),
        in_specs=[any_spec] * 9,
        out_specs=pl.BlockSpec(memory_space=pltpu.VMEM),
        scratch_shapes=[
            pltpu.VMEM((slots, 2, STEP, force_count, resp), BF16),
            pltpu.VMEM((force_count // 128, 2, wave_count, 128), F32),
            pltpu.VMEM((axle_count, case_count), jnp.int32),
            pltpu.VMEM((axle_count, case_count), F32),
            pltpu.VMEM((slot_count, building_count), jnp.int32),
            pltpu.VMEM((building_count // 128, 128), jnp.int32),
            pltpu.VMEM(coupling.shape, BF16),
            pltpu.VMEM(low_table.shape[1:], F32),
            pltpu.VMEM(high_table.shape[1:], F32),
            pltpu.VMEM((HALF, 2 * wave_count), BF16),
            pltpu.VMEM((HALF, 2 * wave_count), BF16),
            pltpu.VMEM((building_count, GROUP), BF16),
            pltpu.VMEM((building_count, GROUP), BF16),
            pltpu.VMEM((building_count * slot_count // GROUP, GROUP), F32),
            pltpu.VMEM((2, building_count, HALF), BF16),
            pltpu.VMEM((building_count, 2 * wave_count), F32),
            pltpu.VMEM((2, case_count, HALF), F32),
            pltpu.VMEM((2 * case_count, 2 * wave_count), BF16),
            pltpu.VMEM((wave_count, resp), F32),
            pltpu.VMEM((case_count, building_count), F32),
            pltpu.SemaphoreType.DMA((7 + force_count // 128,)),
            pltpu.SemaphoreType.DMA((slots,)),
        ],
        compiler_params=pltpu.CompilerParams(vmem_limit_bytes=60 * 1024 * 1024),
    )(
        green.reshape(2, block, 2, force_count, resp),
        rough,
        axle_pos.T,
        axle_load.T,
        rows.T,
        counts.reshape(building_count // 128, 128),
        coupling,
        jnp.asarray(low_table),
        jnp.asarray(high_table),
    )
    arrived = lax.all_to_all(partial_sum, ("wave", "dof"), 0, 0)
    return jnp.sum(arrived.astype(F32), axis=0).T


def solution(mesh):
    in_specs = (
        P(None, "wave", None, "dof"),
        P(None, "wave", None),
        P(),
        P(),
        P(),
        P(),
        P(None, "dof"),
    )
    out_specs = P("dof", "wave")
    return jax.shard_map(body, mesh=mesh, in_specs=in_specs, out_specs=out_specs, check_vma=False)
```

time: 56.6 us -> 45.6 us (0.81)
  Pallas kernels: 37.8 us -> 26.8 us
    pallas_call x1, Pallas kernels: 37.8 us -> 26.8 us  [body(): pl.pallas_call(functools.partial(kernel, (wave_size, dof_size)), out_shap...]
where the time goes in v2:
time: 45.6 us; the launch traced here: 45.4 us
  Pallas kernels  26.8 us (59%)
  blocking collectives  17.9 us (39%)
  other arithmetic  0.65 us (1%)
    pallas_call x1, Pallas kernels, body(): pl.pallas_call(functools.partial(kernel, (wave_size, dof_size)), out_shap...  26.8 us
    all_to_all x1, blocking collectives, body(): arrived = lax.all_to_all(partial_sum, ('wave', 'dof'), 0, 0)  17.9 us

profile of v2, /device:TPU:0, one launch (start us, length us, event | category | flops | bytes accessed | tf_op | source)
XLA Modules:
  0.0 45.4 jit_solution(8819509557002070083)
XLA Ops:
  0.0 26.8 %shard_map.91 = bf16[32,16,256]{2,1,0:T(8,128)(2,1)} custom-call(bf16[2,128,2,512,128]{4,3,2,1,0:T(8,128)(2,1)} %bitcast.green, f32[2,256,512]{2,1,0:T(8,128)} %rough.1, s32[32,128]{1,0:T(8,128)} %bitcast.7, f32[32,128]{1,0:T(8,128)} %bitcast.8, s32[16,1024]{1,0:T(8,128)} %bitcast.6, s32[8,128]{1,0:T(8,128)} %bitcast.9, bf16[1024,128]{1,0:T(8,128)(2,1)} %coupling.1, ...), custom_call_target="tpu_custom_call" | custom-call | tf_op jit(solution)/shard_map/pallas_call | solution.py:329
  26.8 17.9 %all_to_all.5 = bf16[32,16,256]{2,1,0:T(8,128)(2,1)S(1)} all-to-all(bf16[32,16,256]{2,1,0:T(8,128)(2,1)} %shard_map.91), channel_id=1, replica_groups=mesh['wave'=8,'dof'=4] {'wave','dof'}, dimensions={0} | all-to-all | bytes 524288 | tf_op jit(solution)/shard_map/all_to_all | solution.py:370
  44.7 0.7 %convert_reduce_fusion = f32[16,256]{1,0:T(8,128)} fusion(bf16[32,16,256]{2,1,0:T(8,128)(2,1)S(1)} %all_to_all.5), kind=kLoop, calls=%fused_computation | loop fusion | flops 258048 | bytes 278528 | tf_op jit(solution)/shard_map/reduce_sum | solution.py:371

commit v3 on v2

--- a/solution.py
+++ b/solution.py
@@ -15,7 +15,7 @@
 HIGH = HALF // LOW
 GROUP = 256
 STEP = 8
-AHEAD = 4
+AHEAD = 6
 
 F32 = jnp.float32
 BF16 = jnp.bfloat16
@@ -48,13 +48,15 @@
         both = np.stack([np.cos(angle), -np.sin(angle)], axis=3) * scale
         return both.reshape(wave_size, len(stations), 2 * wave_count).astype(np.float32)
 
-    return one(np.arange(LOW), 1.0 / math.sqrt(K)), one(np.arange(HIGH) * LOW, 1.0)
+    return one(np.arange(LOW), 1.0 / math.sqrt(K)), one(np.arange(HIGH) * LOW, 1.0)[:, :, None]
 
 
 def one_hot_rows(key, weights, dtype):
     zero = jnp.zeros(key.shape, dtype)
     parts = [
-        jnp.where(key == jnp.full(key.shape, h, dtype), w, zero) for w in weights for h in range(HIGH)
+        jnp.where(key == jnp.full(key.shape, h + 1, dtype), w, zero)
+        for w in weights
+        for h in range(2 * HIGH)
     ]
     return jnp.concatenate(parts, axis=0)
 
@@ -74,11 +76,16 @@
     return jnp.where(own, dot_nn(values.astype(BF16), copies), 0.0)
 
 
+def item_sums(values, per_sum):
+    rows = values.shape[0]
+    shape = (rows // per_sum, rows)
+    member = jnp.where(iota(shape, 1) // per_sum == iota(shape, 0), 1.0, 0.0)
+    return dot_nn(member.astype(BF16), values.astype(BF16))
+
+
 def station_parts(x):
-    top = x >= HALF
-    sign = jnp.where(top, -1.0, 1.0)
-    high = lax.shift_right_logical(x, LOW.bit_length() - 1) & (HIGH - 1)
-    return sign, (high + 1).astype(F32), (x & (LOW - 1)).astype(F32)
+    high = lax.shift_right_logical(x, LOW.bit_length() - 1)
+    return (high + 1).astype(F32), (x & (LOW - 1)).astype(F32)
 
 
 def kernel(
@@ -105,8 +112,10 @@
     table_hi,
     table_lo,
     key_v,
-    sign_v,
     low_key_v,
+    key_c_v,
+    low_key_c_v,
+    load_parts_v,
     occupancy,
     weights_v,
     loads,
@@ -121,7 +130,9 @@
     slot_count, building_count = rows.shape
     axle_count, case_count = axle_pos.shape
     steps = 2 * block // STEP
-    held = steps // 2
+    early = 3 * steps // 8
+    rounds = building_count // (8 * (GROUP // slot_count))
+    assert rounds == HIGH == case_count // (2 * (GROUP // axle_count))
     slots = ring.shape[0]
     wave = lax.axis_index("wave")
 
@@ -154,7 +165,14 @@
             green.at[:, at, step // per_block], ring.at[slot], ring_sem.at[slot]
         )
 
-    for step in range(held):
+    def pump(step):
+        green_copy(step).wait()
+
+        @pl.when(step + AHEAD < steps)
+        def _():
+            green_copy(step + AHEAD).start()
+
+    for step in range(AHEAD):
         green_copy(jnp.int32(step)).start()
     for copy in small[:2]:
         copy.wait()
@@ -162,71 +180,79 @@
     items = GROUP // slot_count
     for k in range(building_count // 128):
         at = slice(128 * k, 128 * (k + 1))
-        sign, high, low = station_parts(rows_v[:, at])
+        high, low = station_parts(rows_v[:, at])
         used = iota((slot_count, 128), 0) < counts_v[k : k + 1, :]
         key_v[at, :] = spread(jnp.where(used, high, 0.0).T, slot_count).astype(BF16)
-        sign_v[at, :] = spread(sign.T, slot_count).astype(BF16)
         groups = 128 // items
-        member = jnp.where(iota((groups, 128), 1) // items == iota((groups, 128), 0), 1.0, 0.0)
-        low_key_v[groups * k : groups * (k + 1), :] = dot_nn(
-            member.astype(BF16), spread(low.T, slot_count).astype(BF16)
-        )
-
-    @pl.loop(0, building_count // (8 * items))
+        low_key_v[groups * k : groups * (k + 1), :] = item_sums(spread(low.T, slot_count), items)
+    for copy in small[2:6]:
+        copy.wait()
+    items_c = GROUP // axle_count
+    high, low = station_parts(pos_v[...])
+    key_c_v[...] = spread(high.T, axle_count)
+    low = item_sums(spread(low.T, axle_count), items_c)
+    for r in range(rounds):
+        low_key_c_v[r] = low[2 * r : 2 * r + 2]
+    for k, part in enumerate(split(load_v[...])):
+        load_parts_v[k] = spread(part.astype(F32).T, axle_count)
+
+    @pl.loop(0, rounds, unroll=2)
     def _(r):
+        @pl.when(r < early)
+        def _():
+            pump(r)
+
         low_eight = low_key_v[pl.ds(pl.multiple_of(r * 8, 8), 8), :]
         for k in range(8):
             at = pl.ds(pl.multiple_of((r * 8 + k) * items, items), items)
-            key = key_v[at, :] - jnp.ones((items, GROUP), BF16)
-            hot = one_hot_rows(key, [jnp.ones((items, GROUP), BF16), sign_v[at, :]], BF16)
-            low = low_eight[k : k + 1, :].astype(BF16)
-            found = dot_nt(hot, low_rows(low, BF16)).astype(BF16)
-            for h in range(HIGH):
-                for top in range(2):
-                    row = (top * HIGH + h) * items
-                    occupancy[top, at, h * LOW : (h + 1) * LOW] = found[row : row + items]
-
-    for copy in small[2:6]:
-        copy.wait()
-
-    for h in range(HIGH):
-        at = slice(h * LOW, (h + 1) * LOW)
+            hot = one_hot_rows(key_v[at, :], [jnp.ones((items, GROUP), BF16)], BF16)
+            found = dot_nt(hot, low_rows(low_eight[k : k + 1, :].astype(BF16), BF16))
+            half = HIGH * items
+            both = ((found[:half] + found[half:]).astype(BF16), (found[:half] - found[half:]).astype(BF16))
+            for q in range(2):
+                for h in range(HIGH):
+                    occupancy[q, at, h * LOW : (h + 1) * LOW] = both[q][h * items : (h + 1) * items]
+
+        at = pl.ds(pl.multiple_of(r * LOW, LOW), LOW)
         for q in range(2):
             re = slice(2 * q * block, (2 * q + 1) * block)
             im = slice((2 * q + 1) * block, (2 * q + 2) * block)
             low_re, low_im = low_v[:, re], low_v[:, im]
-            high_re, high_im = high_v[h : h + 1, re], high_v[h : h + 1, im]
+            high_re, high_im = high_v[r, :, re], high_v[r, :, im]
             table_hi[at, re], table_lo[at, re] = split(low_re * high_re - low_im * high_im)
             table_hi[at, im], table_lo[at, im] = split(low_re * high_im + low_im * high_re)
 
-    for step in range(held, held + AHEAD):
-        green_copy(jnp.int32(step)).start()
-
-    @pl.loop(0, building_count // 256)
+        low_two = low_key_c_v[r]
+        for k in range(2):
+            at = pl.ds(pl.multiple_of((2 * r + k) * items_c, items_c), items_c)
+            hot = one_hot_rows(key_c_v[at, :], [load_parts_v[0, at, :], load_parts_v[1, at, :]], F32)
+            found = dot_nt(hot.astype(BF16), low_rows(low_two[k : k + 1], F32).astype(BF16))
+            half = HIGH * items_c
+            found = found[: 2 * half] + found[2 * half :]
+            both = (found[:half] + found[half:], found[:half] - found[half:])
+            for q in range(2):
+                for h in range(HIGH):
+                    loads[q, at, h * LOW : (h + 1) * LOW] = both[q][h * items_c : (h + 1) * items_c]
+
+    late = list(range(min(rounds, early), early))
+
+    def pump_late(count):
+        for step in late[:count]:
+            pump(jnp.int32(step))
+        del late[:count]
+
+    pump_late(1)
+
+    @pl.loop(0, building_count // 256, unroll=True)
     def _(r):
         at = pl.ds(pl.multiple_of(r * 256, 256), 256)
         for q in range(2):
             cols = slice(2 * q * block, (2 * q + 2) * block)
             weights_v[at, cols] = dot_nn(occupancy[q, at, :], table_hi[:, cols])
 
-    sign, high, low = station_parts(pos_v[...])
-    high = spread(high.T, axle_count) - 1.0
-    low = spread(low.T, axle_count)
-    load_parts = []
-    for part in split(load_v[...]):
-        load_parts += [part.astype(F32), sign * part.astype(F32)]
-    load_parts = [spread(part.T, axle_count) for part in load_parts]
-    items_c = GROUP // axle_count
-    for g in range(case_count // items_c):
-        at = slice(g * items_c, (g + 1) * items_c)
-        hot = one_hot_rows(high[at], [part[at] for part in load_parts], F32)
-        row = jnp.sum(low[at], axis=0, keepdims=True)
-        found = dot_nt(hot.astype(BF16), low_rows(row, F32).astype(BF16))
-        found = found[: 2 * HIGH * items_c] + found[2 * HIGH * items_c :]
-        for top in range(2):
-            for h in range(HIGH):
-                row = (top * HIGH + h) * items_c
-                loads[top, at, h * LOW : (h + 1) * LOW] = found[row : row + items_c]
+    pump_late(1)
+
+    pump_late(1)
     for q in range(2):
         cols = slice(2 * q * block, (2 * q + 2) * block)
         load_hi, load_lo = split(loads[q])
@@ -239,13 +265,6 @@
 
     for copy in small[6:]:
         copy.wait()
-
-    def pump(step):
-        green_copy(step).wait()
-
-        @pl.when(step + AHEAD < steps)
-        def _():
-            green_copy(step + AHEAD).start()
 
     def one_step(step, q):
         slot = lax.rem(step, slots)
@@ -272,25 +291,27 @@
             prod = dot_nn(left, right)
             g_re = jnp.where(rank == k, prod[:STEP] + prod[2 * STEP : 3 * STEP], g_re)
             g_im = jnp.where(rank == k, prod[STEP : 2 * STEP] + prod[3 * STEP :], g_im)
-        g_v[pl.ds(row, STEP), :] = g_re
-        g_v[pl.ds(block + row, STEP), :] = g_im
-
-    for step in range(held):
-        green_copy(jnp.int32(step)).wait()
-
+        g_v[q, pl.ds(row, STEP), :] = g_re
+        g_v[q, pl.ds(block + row, STEP), :] = g_im
+
+    pump_late(early)
     owned_cases = case_count // wave_size
     owned_buildings = building_count // dof_size
     per_tile = owned_buildings // 128
     for q in range(2):
 
-        @pl.loop(q * steps // 8, (q + 1) * steps // 8)
-        def _(r):
-            for k in range(4):
-                if k % 2:
-                    pump(held + 2 * r + k // 2)
-                one_step(4 * r + k, q)
-
-        g_both = jnp.concatenate(split(g_v[...]), axis=1)
+        def eight_steps(r, q=q):
+            for k in range(8):
+                if k >= 3:
+                    pump(early + 5 * r + k - 3)
+                one_step(8 * r + k, q + k // 4 if steps < 16 else q)
+
+        if steps >= 16:
+            pl.loop(q * steps // 16, (q + 1) * steps // 16)(eight_steps)
+        elif q == 0:
+            eight_steps(jnp.int32(0))
+
+        g_both = jnp.concatenate(split(g_v[q]), axis=1)
         re = slice(2 * q * block, (2 * q + 1) * block)
         im = slice((2 * q + 1) * block, (2 * q + 2) * block)
         phase_q = phase_v[:, 2 * q * block : (2 * q + 2) * block]
@@ -301,9 +322,9 @@
             h_re, h_im = h[:, :block], h[:, block:]
             w_re, w_im = weights_v[at, re], weights_v[at, im]
             both = jnp.concatenate([w_re * h_re + w_im * h_im, w_im * h_re - w_re * h_im], axis=1)
-            both_hi, both_lo = split(both)
+            both_hi = both.astype(BF16)
             prod = dot_nt(phase_q, both_hi)
-            part = prod[:case_count] + prod[case_count:] + dot_nt(phase_q[:case_count], both_lo)
+            part = prod[:case_count] + prod[case_count:]
             if q == 0:
                 total[:, at] = part
                 continue
@@ -323,7 +344,7 @@
     case_count, axle_count = axle_pos.shape
     block = wave_count // 2
     low_table, high_table = factor_tables(wave_size, wave_count)
-    slots = block // STEP + AHEAD
+    slots = 3 * wave_count // (8 * STEP) + AHEAD
     owned = (case_count // wave_size, building_count // dof_size)
     any_spec = pl.BlockSpec(memory_space=pl.ANY)
     partial_sum = pl.pallas_call(
@@ -344,13 +365,15 @@
             pltpu.VMEM((HALF, 2 * wave_count), BF16),
             pltpu.VMEM((HALF, 2 * wave_count), BF16),
             pltpu.VMEM((building_count, GROUP), BF16),
-            pltpu.VMEM((building_count, GROUP), BF16),
             pltpu.VMEM((building_count * slot_count // GROUP, GROUP), F32),
+            pltpu.VMEM((case_count, GROUP), F32),
+            pltpu.VMEM((HIGH, 2, GROUP), F32),
+            pltpu.VMEM((2, case_count, GROUP), F32),
             pltpu.VMEM((2, building_count, HALF), BF16),
             pltpu.VMEM((building_count, 2 * wave_count), F32),
             pltpu.VMEM((2, case_count, HALF), F32),
             pltpu.VMEM((2 * case_count, 2 * wave_count), BF16),
-            pltpu.VMEM((wave_count, resp), F32),
+            pltpu.VMEM((2, wave_count, resp), F32),
             pltpu.VMEM((case_count, building_count), F32),
             pltpu.SemaphoreType.DMA((7 + force_count // 128,)),
             pltpu.SemaphoreType.DMA((slots,)),

time: 45.6 us -> 42.8 us (0.939)
  Pallas kernels: 26.8 us -> 24 us
    pallas_call x1, Pallas kernels: 26.8 us -> 24 us  [body(): pl.pallas_call(functools.partial(kernel, (wave_size, dof_size)), out_shap...]
where the time goes in v3:
time: 42.8 us; the launch traced here: 42.6 us
  Pallas kernels  24 us (56%)
  blocking collectives  17.9 us (42%)
  other arithmetic  0.65 us (2%)
    pallas_call x1, Pallas kernels, body(): pl.pallas_call(functools.partial(kernel, (wave_size, dof_size)), out_shap...  24 us
    all_to_all x1, blocking collectives, body(): arrived = lax.all_to_all(partial_sum, ('wave', 'dof'), 0, 0)  17.9 us

profile of v3, /device:TPU:0, one launch (start us, length us, event | category | flops | bytes accessed | tf_op | source)
XLA Modules:
  0.0 42.6 jit_solution(4817342824608231888)
XLA Ops:
  0.0 24.0 %shard_map.91 = bf16[32,16,256]{2,1,0:T(8,128)(2,1)} custom-call(bf16[2,128,2,512,128]{4,3,2,1,0:T(8,128)(2,1)} %bitcast.green, f32[2,256,512]{2,1,0:T(8,128)} %rough.1, s32[32,128]{1,0:T(8,128)} %bitcast.7, f32[32,128]{1,0:T(8,128)} %bitcast.8, s32[16,1024]{1,0:T(8,128)} %bitcast.6, s32[8,128]{1,0:T(8,128)} %bitcast.9, bf16[1024,128]{1,0:T(8,128)(2,1)} %coupling.1, ...), custom_call_target="tpu_custom_call" | custom-call | tf_op jit(solution)/shard_map/pallas_call | solution.py:350
  24.1 17.9 %all_to_all.5 = bf16[32,16,256]{2,1,0:T(8,128)(2,1)S(1)} all-to-all(bf16[32,16,256]{2,1,0:T(8,128)(2,1)} %shard_map.91), channel_id=1, replica_groups=mesh['wave'=8,'dof'=4] {'wave','dof'}, dimensions={0} | all-to-all | bytes 524288 | tf_op jit(solution)/shard_map/all_to_all | solution.py:393
  42.0 0.7 %convert_reduce_fusion = f32[16,256]{1,0:T(8,128)} fusion(bf16[32,16,256]{2,1,0:T(8,128)(2,1)S(1)} %all_to_all.5), kind=kLoop, calls=%fused_computation | loop fusion | flops 258048 | bytes 278528 | tf_op jit(solution)/shard_map/reduce_sum | solution.py:394

commit v4 on v3

--- a/solution.py
+++ b/solution.py
@@ -122,6 +122,7 @@
     phase_v,
     g_v,
     total,
+    out_v,
     small_sem,
     ring_sem,
 ):
@@ -296,6 +297,10 @@
 
     pump_late(early)
     owned_cases = case_count // wave_size
+
+    def out_copy(d):
+        return pltpu.make_async_copy(out_v.at[d], out.at[:, d], small_sem.at[d])
+
     owned_buildings = building_count // dof_size
     per_tile = owned_buildings // 128
     for q in range(2):
@@ -333,7 +338,10 @@
             )
             part = (total[:, at] + part) * (1.0 / count.astype(F32))
             for w in range(wave_size):
-                out[w * dof_size + d] = part[w * owned_cases : (w + 1) * owned_cases].astype(BF16)
+                out_v[d, w] = part[w * owned_cases : (w + 1) * owned_cases].astype(BF16)
+            out_copy(d).start()
+    for d in range(dof_size):
+        out_copy(d).wait()
 
 
 def body(green, rough, axle_pos, axle_load, rows, counts, coupling):
@@ -349,9 +357,9 @@
     any_spec = pl.BlockSpec(memory_space=pl.ANY)
     partial_sum = pl.pallas_call(
         functools.partial(kernel, (wave_size, dof_size)),
-        out_shape=jax.ShapeDtypeStruct((wave_size * dof_size, *owned), BF16),
+        out_shape=jax.ShapeDtypeStruct((wave_size, dof_size, *owned), BF16),
         in_specs=[any_spec] * 9,
-        out_specs=pl.BlockSpec(memory_space=pltpu.VMEM),
+        out_specs=any_spec,
         scratch_shapes=[
             pltpu.VMEM((slots, 2, STEP, force_count, resp), BF16),
             pltpu.VMEM((force_count // 128, 2, wave_count, 128), F32),
@@ -375,6 +383,7 @@
             pltpu.VMEM((2 * case_count, 2 * wave_count), BF16),
             pltpu.VMEM((2, wave_count, resp), F32),
             pltpu.VMEM((case_count, building_count), F32),
+            pltpu.VMEM((dof_size, wave_size, *owned), BF16),
             pltpu.SemaphoreType.DMA((7 + force_count // 128,)),
             pltpu.SemaphoreType.DMA((slots,)),
         ],
@@ -390,7 +399,9 @@
         jnp.asarray(low_table),
         jnp.asarray(high_table),
     )
-    arrived = lax.all_to_all(partial_sum, ("wave", "dof"), 0, 0)
+    arrived = lax.all_to_all(
+        partial_sum.reshape(wave_size * dof_size, *owned), ("wave", "dof"), 0, 0
+    )
     return jnp.sum(arrived.astype(F32), axis=0).T
 
 

time: 42.8 us -> 42.8 us (level)
  no operation moved by 1% of the time
where the time goes in v4:
time: 42.8 us; the launch traced here: 42.6 us
  Pallas kernels  24 us (56%)
  blocking collectives  17.9 us (42%)
  other arithmetic  0.65 us (2%)
    pallas_call x1, Pallas kernels, body(): pl.pallas_call(functools.partial(kernel, (wave_size, dof_size)), out_shap...  24 us
    all_to_all x1, blocking collectives, body(): lax.all_to_all(partial_sum.reshape(wave_size * dof_size, *owned), ('wave'...  17.9 us

profile of v4, /device:TPU:0, one launch (start us, length us, event | category | flops | bytes accessed | tf_op | source)
XLA Modules:
  0.0 42.6 jit_solution(7288493429850949376)
XLA Ops:
  0.0 24.0 %shard_map.91 = bf16[8,4,16,256]{3,2,1,0:T(8,128)(2,1)} custom-call(bf16[2,128,2,512,128]{4,3,2,1,0:T(8,128)(2,1)} %bitcast.green, f32[2,256,512]{2,1,0:T(8,128)} %rough.1, s32[32,128]{1,0:T(8,128)} %bitcast.9, f32[32,128]{1,0:T(8,128)} %bitcast.10, s32[16,1024]{1,0:T(8,128)} %bitcast.8, s32[8,128]{1,0:T(8,128)} %bitcast.11, bf16[1024,128]{1,0:T(8,128)(2,1)} %coupling.1, ...), custom_call_target="tpu_custom_call" | custom-call | tf_op jit(solution)/shard_map/pallas_call | solution.py:358
  24.0 17.9 %all_to_all.5 = bf16[32,16,256]{2,1,0:T(8,128)(2,1)S(1)} all-to-all(bf16[32,16,256]{2,1,0:T(8,128)(2,1)} %bitcast.7), channel_id=1, replica_groups=mesh['wave'=8,'dof'=4] {'wave','dof'}, dimensions={0} | all-to-all | bytes 524288 | tf_op jit(solution)/shard_map/all_to_all | solution.py:402
  41.9 0.7 %convert_reduce_fusion = f32[16,256]{1,0:T(8,128)} fusion(bf16[32,16,256]{2,1,0:T(8,128)(2,1)S(1)} %all_to_all.5), kind=kLoop, calls=%fused_computation | loop fusion | flops 258048 | bytes 278528 | tf_op jit(solution)/shard_map/reduce_sum | solution.py:405
